TPU v7x, 256 devices: a whole 4x4x8 slice. The times are simulated.
256 devices in a mesh: grp: 8 (over y, z_lo), row: 32 (over z_hi, x, core).
Axes of the slice: x: 4, y: 4, z: 8 (z_hi: 4, z_lo: 2; z = z_hi * 2 + z_lo), core: 2. Of those that a mesh axis runs over, the one named last changes fastest.
Arguments:
- matrix: float32 [1048576, 256], P(('grp', 'row')), may hold values from -6 to 6
- row_signs: int32 [1048576], P(('grp', 'row')), may hold values from -1 to 1, as said below
- block_dest: int32 [8192], P(('grp', 'row')), may hold values from 0 to 15
- block_signs: int32 [8192], P(('grp', 'row')), may hold values from -1 to 1, as said below
Outputs:
- sketch: float32 [2048, 256], P('row')
Inputs may be any that keep to these rules, and one draw needn't show every extreme that they name: `row_signs`: each entry is -1 or 1. `block_signs`: each entry is -1 or 1.
All inputs are finite; a program needn't handle non-finite values.
Results may differ from a plain program's by a relative error of at most 0.0003.
Values sent between devices are 32-bit elements; how exact they have to be, the bound alone decides.
No kernel may reach another device: no remote copies, remote signals or barrier semaphores. Data moves between devices by JAX's collectives and lax.ppermute only.
A program may use at most 64 MiB of HBM per device.

v0:
```python
import math
import jax
import jax.numpy as jnp
from jax import lax
from jax.sharding import PartitionSpec as P

SKETCH = 2048


def swapped(array, axis, stride):
    return lax.ppermute(array, axis, [(i, i ^ 1 << stride) for i in range(lax.axis_size(axis))])


def sylvester(order):
    indices = jnp.arange(order, dtype=jnp.int32)
    common = indices[:, None] & indices[None, :]
    parity = jnp.zeros((order, order), jnp.int32)
    for section in range(order.bit_length() - 1):
        parity = parity + (common >> section & 1)
    return (1 - 2 * (parity % 2)).astype(jnp.float32)


def unit_weights(dests, signs, start, piece, block, target_count):
    unit_rows = min(piece, block)
    unit_count = piece // unit_rows
    starts = start + jnp.arange(unit_count, dtype=jnp.int32) * unit_rows
    which_block = starts // block
    offset = starts % block // unit_rows
    dest_sel = jnp.take(dests, which_block, axis=1)
    sign_sel = jnp.take(signs, which_block, axis=1).astype(jnp.float32)
    targets = jnp.arange(target_count, dtype=jnp.int32)
    within = jnp.arange(block // unit_rows, dtype=jnp.int32)
    to_dest = (dest_sel[None, :, :] == targets[:, None, None]).astype(jnp.float32) * sign_sel[
        None, :, :
    ]
    to_slot = (offset[None, :] == within[:, None]).astype(jnp.float32)
    return to_dest[:, None, :, :] * to_slot[None, :, None, :]


def place(weights, held, block):
    sources, piece, columns = held.shape
    unit_rows = min(piece, block)
    grid = held.reshape(sources, piece // unit_rows, unit_rows, columns)
    return jnp.einsum("sjmk,mkuc->sjuc", weights, grid, precision=lax.Precision.HIGHEST)


def body(matrix, row_signs, block_dest, block_signs):
    precise = lax.Precision.HIGHEST
    row_count, col_count = matrix.shape
    block = row_count // block_dest.shape[0]
    target_count = SKETCH // block
    dev_count = lax.axis_size("row")
    my_index = lax.axis_index("row")
    exponent = row_count.bit_length() - 1
    first_size = 1 << exponent // 2
    second_size = row_count // first_size
    signed = matrix * row_signs[:, None].astype(jnp.float32)
    shaped = signed.reshape(first_size, second_size, col_count)
    shaped = jnp.einsum("ya,abc->ybc", sylvester(first_size), shaped, precision=precise)
    shaped = jnp.einsum("zb,abc->azc", sylvester(second_size), shaped, precision=precise)
    mixed = shaped.reshape(row_count, col_count) / math.sqrt(row_count)
    flipped = mixed
    inverse_root = 1.0 / math.sqrt(2.0)
    for section in range(dev_count.bit_length() - 1):
        partner = swapped(flipped, "row", section)
        upper = my_index >> section & 1 == 1
        flipped = jnp.where(upper, partner - flipped, flipped + partner) * inverse_root
    weights = unit_weights(
        block_dest[None, :], block_signs[None, :], 0, row_count, block, target_count
    )
    partial_value = place(weights, flipped[None, :, :], block)
    partial_value = partial_value.reshape(SKETCH, col_count)
    group_count = lax.axis_size("grp")
    share = lax.psum_scatter(partial_value, "row", scatter_dimension=0, tiled=True)
    summed = lax.psum(share, "grp")
    total_rows = row_count * dev_count * group_count
    return summed * math.sqrt(SKETCH / total_rows)


def solution(mesh):
    return jax.shard_map(
        body,
        mesh=mesh,
        in_specs=(P(("grp", "row"), None), P(("grp", "row")), P(("grp", "row")), P(("grp", "row"))),
        out_specs=P("row", None),
        check_vma=False,
    )
```

profile of v0, /device:TPU:2, one launch (start us, length us, event | category | flops | bytes accessed | tf_op | source)
XLA Modules:
  0.0 799.0 jit_solution(16415899795226942938)
XLA Ops:
  6.5 0.0 copy-start
  6.5 0.0 reduce-scatter.2.cloned.1.call-start
  6.5 0.7 convert_element_type.29
  7.3 2.6 broadcast_multiply_fusion
  9.9 6.3 fusion.2
  16.1 7.1 fusion.6
  23.2 0.0 collective-permute-start
  23.3 7.5 collective-permute-done
  30.8 5.9 select_multiply_fusion.4
  36.7 2.3 collective-permute-start.1
  39.0 91.2 %collective-permute-done.1 = f32[4096,256]{1,0:T(8,128)} collective-permute-done((f32[4096,256]{1,0:T(8,128)}, f32[4096,256]{1,0:T(8,128)}, u32[]{:S(2)}, u32[]{:S(2)}) %collective-permute-start.1) | collective-permute-done | bytes 4194336 | tf_op jit(solution)/shard_map/ppermute | solution.py:11
  130.2 5.9 select_multiply_fusion.3
  136.1 1.6 collective-permute-start.2
  137.7 92.3 %collective-permute-done.2 = f32[4096,256]{1,0:T(8,128)} collective-permute-done((f32[4096,256]{1,0:T(8,128)}, f32[4096,256]{1,0:T(8,128)}, u32[]{:S(2)}, u32[]{:S(2)}) %collective-permute-start.2) | collective-permute-done | bytes 4194336 | tf_op jit(solution)/shard_map/ppermute | solution.py:11
  230.0 5.9 select_multiply_fusion.2
  236.0 2.4 collective-permute-start.3
  238.4 0.0 copy-start.1
  238.4 179.9 %collective-permute-done.3 = f32[4096,256]{1,0:T(8,128)} collective-permute-done((f32[4096,256]{1,0:T(8,128)}, f32[4096,256]{1,0:T(8,128)}, u32[]{:S(2)}, u32[]{:S(2)}) %collective-permute-start.3) | collective-permute-done | bytes 4194336 | tf_op jit(solution)/shard_map/ppermute | solution.py:11
  418.3 5.9 select_multiply_fusion.1
  424.2 6.0 collective-permute-start.4
  430.3 0.0 copy-done
  430.3 0.7 gather_fusion
  431.0 0.0 copy-done.1
  431.0 0.7 gather_fusion.1
  431.7 179.9 %collective-permute-done.4 = f32[4096,256]{1,0:T(8,128)} collective-permute-done((f32[4096,256]{1,0:T(8,128)}, f32[4096,256]{1,0:T(8,128)}, u32[]{:S(2)}, u32[]{:S(2)}) %collective-permute-start.4) | collective-permute-done | bytes 4194336 | tf_op jit(solution)/shard_map/ppermute | solution.py:11
  611.6 4.0 select_multiply_fusion
  615.6 4.4 fusion.4
  620.0 2.6 copy.6
  622.6 0.0 reduce-scatter.2.cloned.1.call-update
  622.6 0.0 all-reduce.2.cloned.1.call-start
  622.6 89.8 %reduce-scatter.2.cloned.1.call-done = f32[64,256]{1,0:T(8,128)} async-done(((f32[2048,256]{1,0:T(8,128)}), f32[64,256]{1,0:T(8,128)}) %reduce-scatter.2.cloned.1.call-update) | async-done | bytes 65552 | tf_op jit(solution)/shard_map/reduce_scatter | solution.py:74
  712.4 0.0 all-reduce.2.cloned.1.call-update
  712.5 78.2 %all-reduce.2.cloned.1.call-done = f32[64,256]{1,0:T(8,128)} async-done(((f32[64,256]{1,0:T(8,128)}), f32[64,256]{1,0:T(8,128)}) %all-reduce.2.cloned.1.call-update) | async-done | bytes 65552 | tf_op jit(solution)/shard_map/psum | solution.py:75
  790.7 1.5 broadcast_multiply_fusion.1
  (4 shorter events, 0.1 us)
Async XLA Ops:
  6.5 423.7 %copy-start = (s32[32]{0:T(128)S(1)}, s32[32]{0:T(128)}, u32[]{:S(2)}) copy-start(s32[32]{0:T(128)} %param.8) | copy-start | bytes 388
  6.5 705.9 %reduce-scatter.2.cloned.1.call-start = ((), (), s32[]{:S(2)}) async-start(), calls=%async_computation.1 | async-start | bytes 2162688 | tf_op jit(solution)/shard_map/reduce_scatter | solution.py:74
  23.2 7.5 collective-permute-start
  36.7 93.5 %collective-permute-start.1 = (f32[4096,256]{1,0:T(8,128)}, f32[4096,256]{1,0:T(8,128)}, u32[]{:S(2)}, u32[]{:S(2)}) collective-permute-start(f32[4096,256]{1,0:T(8,128)} %select_multiply_fusion.4), channel_id=1, source_target_pairs={{0,2},{1,3},{2,0},{3,1},{4,6},{5,7},{6,4},{7,5},{8,10},{9,11},{10,... | collective-permute-start | bytes 12582920 | tf_op jit(solution)/shard_map/ppermute | solution.py:11
  136.1 93.9 %collective-permute-start.2 = (f32[4096,256]{1,0:T(8,128)}, f32[4096,256]{1,0:T(8,128)}, u32[]{:S(2)}, u32[]{:S(2)}) collective-permute-start(f32[4096,256]{1,0:T(8,128)} %select_multiply_fusion.3), channel_id=1, source_target_pairs={{0,4},{1,5},{2,6},{3,7},{4,0},{5,1},{6,2},{7,3},{8,12},{9,13},{10,... | collective-permute-start | bytes 12582920 | tf_op jit(solution)/shard_map/ppermute | solution.py:11
  236.0 182.3 %collective-permute-start.3 = (f32[4096,256]{1,0:T(8,128)}, f32[4096,256]{1,0:T(8,128)}, u32[]{:S(2)}, u32[]{:S(2)}) collective-permute-start(f32[4096,256]{1,0:T(8,128)} %select_multiply_fusion.2), channel_id=1, source_target_pairs={{0,8},{1,9},{2,10},{3,11},{4,12},{5,13},{6,14},{7,15},{8,0},{9,1},... | collective-permute-start | bytes 12582920 | tf_op jit(solution)/shard_map/ppermute | solution.py:11
  238.4 192.6 %copy-start.1 = (s32[32]{0:T(128)S(1)}, s32[32]{0:T(128)}, u32[]{:S(2)}) copy-start(s32[32]{0:T(128)} %param.9) | copy-start | bytes 388
  424.2 187.4 %collective-permute-start.4 = (f32[4096,256]{1,0:T(8,128)}, f32[4096,256]{1,0:T(8,128)}, u32[]{:S(2)}, u32[]{:S(2)}) collective-permute-start(f32[4096,256]{1,0:T(8,128)} %select_multiply_fusion.1), channel_id=1, source_target_pairs={{0,16},{1,17},{2,18},{3,19},{4,20},{5,21},{6,22},{7,23},{8,24},{9,... | collective-permute-start | bytes 12582920 | tf_op jit(solution)/shard_map/ppermute | solution.py:11
  622.6 168.1 %all-reduce.2.cloned.1.call-start = ((), (), s32[]{:S(2)}) async-start(), calls=%async_computation.2 | async-start | bytes 131072 | tf_op jit(solution)/shard_map/psum | solution.py:75
Sparse Core Ops, SparseCore 0:
  622.7 89.6 reduce-scatter.1
  715.0 75.5 all-reduce.1
where the time goes:
time: 799 us
  waiting for transfers between devices  719 us (90%)
  other arithmetic  32.6 us (4%)
  matrix products  17.8 us (2%)
  between operations  13.5 us (2%)
  starting transfers between devices  12.4 us (2%)
    ppermute x5, waiting for transfers between devices, swapped(): lax.ppermute(array, axis, [(i, i ^ 1 << stride) for i in range(lax.axis_s...  551 us
    reduce_scatter x1, waiting for transfers between devices, body(): lax.psum_scatter(partial_value, 'row', scatter_dimension=0, tiled=True)  89.8 us
    psum x1, waiting for transfers between devices, body(): summed = lax.psum(share, 'grp')  78.2 us
    mul x5, other arithmetic, body(): jnp.where(upper, partner - flipped, flipped + partner) * inverse_root  27.8 us
  transfers between devices with their start and end apart: 7, of which 7 were waited for; matrix products, arithmetic and copies ran while one was open for 0% of the time, Pallas kernels for 0%

commit v1 on v0

--- a/solution.py
+++ b/solution.py
@@ -72,7 +72,11 @@
     partial_value = partial_value.reshape(SKETCH, col_count)
     group_count = lax.axis_size("grp")
     share = lax.psum_scatter(partial_value, "row", scatter_dimension=0, tiled=True)
-    summed = lax.psum(share, "grp")
+
+    def finish_the_surface(sample):
+        return jnp.sum(lax.all_gather(sample, "grp"), 0)
+
+    summed = finish_the_surface(share)
     total_rows = row_count * dev_count * group_count
     return summed * math.sqrt(SKETCH / total_rows)
 

time: 799 us -> 750 us (0.939)
  waiting for transfers between devices: 719 us -> 641 us
  blocking collectives: 0 us -> 30.3 us
    psum x1 -> x0, waiting for transfers between devices: 78.2 us -> none  [body(): summed = lax.psum(share, 'grp')]
    all_gather x0 -> x1, blocking collectives: none -> 30.3 us  [finish_the_surface(): return jnp.sum(lax.all_gather(sample, 'grp'), 0)]
  transfers between devices with their start and end apart: 7 -> 6, of which waited for: 7 -> 6; matrix products, arithmetic and copies ran while one was open for 0% -> 0% of each run, Pallas kernels for 0% -> 0%
where the time goes in v1:
time: 750 us
  waiting for transfers between devices  641 us (85%)
  other arithmetic  31.8 us (4%)
  blocking collectives  30.3 us (4%)
  matrix products  17.8 us (2%)
  between operations  13.5 us (2%)
  starting transfers between devices  12.3 us (2%)
    ppermute x5, waiting for transfers between devices, swapped(): lax.ppermute(array, axis, [(i, i ^ 1 << stride) for i in range(lax.axis_s...  551 us
    reduce_scatter x1, waiting for transfers between devices, body(): lax.psum_scatter(partial_value, 'row', scatter_dimension=0, tiled=True)  89.8 us
    all_gather x1, blocking collectives, finish_the_surface(): return jnp.sum(lax.all_gather(sample, 'grp'), 0)  30.3 us
    mul x5, other arithmetic, body(): jnp.where(upper, partner - flipped, flipped + partner) * inverse_root  27.8 us
  transfers between devices with their start and end apart: 6, of which 6 were waited for; matrix products, arithmetic and copies ran while one was open for 0% of the time, Pallas kernels for 0%

profile of v1, /device:TPU:2, one launch (start us, length us, event | category | flops | bytes accessed | tf_op | source)
XLA Modules:
  0.0 750.2 jit_solution(14833899902822461225)
XLA Ops:
  6.5 0.0 copy-start
  6.5 0.0 reduce-scatter.2.cloned.1.call-start
  6.5 0.7 convert_element_type.29
  7.3 2.6 broadcast_multiply_fusion
  9.9 6.3 fusion.2
  16.1 7.1 fusion.6
  23.2 0.0 collective-permute-start
  23.2 7.5 collective-permute-done
  30.7 5.9 select_multiply_fusion.4
  36.7 2.3 collective-permute-start.1
  39.0 91.2 %collective-permute-done.1 = f32[4096,256]{1,0:T(8,128)} collective-permute-done((f32[4096,256]{1,0:T(8,128)}, f32[4096,256]{1,0:T(8,128)}, u32[]{:S(2)}, u32[]{:S(2)}) %collective-permute-start.1) | collective-permute-done | bytes 4194336 | tf_op jit(solution)/shard_map/ppermute | solution.py:11
  130.1 5.9 select_multiply_fusion.3
  136.1 1.6 collective-permute-start.2
  137.7 92.3 %collective-permute-done.2 = f32[4096,256]{1,0:T(8,128)} collective-permute-done((f32[4096,256]{1,0:T(8,128)}, f32[4096,256]{1,0:T(8,128)}, u32[]{:S(2)}, u32[]{:S(2)}) %collective-permute-start.2) | collective-permute-done | bytes 4194336 | tf_op jit(solution)/shard_map/ppermute | solution.py:11
  230.0 5.9 select_multiply_fusion.2
  235.9 2.4 collective-permute-start.3
  238.4 0.0 copy-start.1
  238.4 179.9 %collective-permute-done.3 = f32[4096,256]{1,0:T(8,128)} collective-permute-done((f32[4096,256]{1,0:T(8,128)}, f32[4096,256]{1,0:T(8,128)}, u32[]{:S(2)}, u32[]{:S(2)}) %collective-permute-start.3) | collective-permute-done | bytes 4194336 | tf_op jit(solution)/shard_map/ppermute | solution.py:11
  418.3 5.9 select_multiply_fusion.1
  424.2 6.0 collective-permute-start.4
  430.2 0.0 copy-done
  430.2 0.7 gather_fusion
  430.9 0.0 copy-done.1
  430.9 0.7 gather_fusion.1
  431.7 179.9 %collective-permute-done.4 = f32[4096,256]{1,0:T(8,128)} collective-permute-done((f32[4096,256]{1,0:T(8,128)}, f32[4096,256]{1,0:T(8,128)}, u32[]{:S(2)}, u32[]{:S(2)}) %collective-permute-start.4) | collective-permute-done | bytes 4194336 | tf_op jit(solution)/shard_map/ppermute | solution.py:11
  611.5 4.0 select_multiply_fusion
  615.6 4.4 fusion.4
  620.0 2.6 copy.6
  622.5 0.0 reduce-scatter.2.cloned.1.call-update
  622.6 89.8 %reduce-scatter.2.cloned.1.call-done = f32[64,256]{1,0:T(8,128)} async-done(((f32[2048,256]{1,0:T(8,128)}), f32[64,256]{1,0:T(8,128)}) %reduce-scatter.2.cloned.1.call-update) | async-done | bytes 65552 | tf_op jit(solution)/shard_map/reduce_scatter | solution.py:74
  712.3 30.3 %all-gather = f32[512,256]{1,0:T(8,128)S(1)} all-gather(f32[64,256]{1,0:T(8,128)} %reduce-scatter.2.cloned.1.call-done), channel_id=2, replica_groups=mesh['grp'=8,'row'=32] {'grp'}, dimensions={0}, use_global_device_ids=true | all-gather | bytes 589824 | tf_op jit(solution)/shard_map/all_gather | solution.py:77
  742.7 0.6 broadcast_multiply_fusion.1
  (5 shorter events, 0.1 us)
Async XLA Ops:
  6.5 423.7 %copy-start = (s32[32]{0:T(128)S(1)}, s32[32]{0:T(128)}, u32[]{:S(2)}) copy-start(s32[32]{0:T(128)} %param.8) | copy-start | bytes 388
  6.5 705.8 %reduce-scatter.2.cloned.1.call-start = ((), (), s32[]{:S(2)}) async-start(), calls=%async_computation.1 | async-start | bytes 2162688 | tf_op jit(solution)/shard_map/reduce_scatter | solution.py:74
  23.2 7.5 %collective-permute-start = (f32[4096,256]{1,0:T(8,128)}, f32[4096,256]{1,0:T(8,128)}, u32[]{:S(2)}, u32[]{:S(2)}) collective-permute-start(f32[4096,256]{1,0:T(8,128)} %bitcast.10), channel_id=1, source_target_pairs={{0,1},{1,0},{2,3},{3,2},{4,5},{5,4},{6,7},{7,6},{8,9},{9,8},{10,11... | collective-permute-start | bytes 12582920 | tf_op jit(solution)/shard_map/ppermute | solution.py:11
  36.7 93.5 %collective-permute-start.1 = (f32[4096,256]{1,0:T(8,128)}, f32[4096,256]{1,0:T(8,128)}, u32[]{:S(2)}, u32[]{:S(2)}) collective-permute-start(f32[4096,256]{1,0:T(8,128)} %select_multiply_fusion.4), channel_id=1, source_target_pairs={{0,2},{1,3},{2,0},{3,1},{4,6},{5,7},{6,4},{7,5},{8,10},{9,11},{10,... | collective-permute-start | bytes 12582920 | tf_op jit(solution)/shard_map/ppermute | solution.py:11
  136.1 93.9 %collective-permute-start.2 = (f32[4096,256]{1,0:T(8,128)}, f32[4096,256]{1,0:T(8,128)}, u32[]{:S(2)}, u32[]{:S(2)}) collective-permute-start(f32[4096,256]{1,0:T(8,128)} %select_multiply_fusion.3), channel_id=1, source_target_pairs={{0,4},{1,5},{2,6},{3,7},{4,0},{5,1},{6,2},{7,3},{8,12},{9,13},{10,... | collective-permute-start | bytes 12582920 | tf_op jit(solution)/shard_map/ppermute | solution.py:11
  235.9 182.3 %collective-permute-start.3 = (f32[4096,256]{1,0:T(8,128)}, f32[4096,256]{1,0:T(8,128)}, u32[]{:S(2)}, u32[]{:S(2)}) collective-permute-start(f32[4096,256]{1,0:T(8,128)} %select_multiply_fusion.2), channel_id=1, source_target_pairs={{0,8},{1,9},{2,10},{3,11},{4,12},{5,13},{6,14},{7,15},{8,0},{9,1},... | collective-permute-start | bytes 12582920 | tf_op jit(solution)/shard_map/ppermute | solution.py:11
  238.4 192.6 %copy-start.1 = (s32[32]{0:T(128)S(1)}, s32[32]{0:T(128)}, u32[]{:S(2)}) copy-start(s32[32]{0:T(128)} %param.9) | copy-start | bytes 388
  424.2 187.4 %collective-permute-start.4 = (f32[4096,256]{1,0:T(8,128)}, f32[4096,256]{1,0:T(8,128)}, u32[]{:S(2)}, u32[]{:S(2)}) collective-permute-start(f32[4096,256]{1,0:T(8,128)} %select_multiply_fusion.1), channel_id=1, source_target_pairs={{0,16},{1,17},{2,18},{3,19},{4,20},{5,21},{6,22},{7,23},{8,24},{9,... | collective-permute-start | bytes 12582920 | tf_op jit(solution)/shard_map/ppermute | solution.py:11
Sparse Core Ops, SparseCore 0:
  622.7 89.6 reduce-scatter.1
